TPU v7x, 32 devices: a whole 2x2x4 slice. The times are simulated.
32 devices in a mesh: dp: 8 (over z, x), seq: 4 (over y, core).
Axes of the slice: x: 2, y: 2, z: 4, core: 2. Of those that a mesh axis runs over, the one named last changes fastest.
Arguments:
- hidden_in: bfloat16 [4096, 1024], P(('dp', 'seq')), may hold values from -6 to 6
- cotangent: bfloat16 [4096, 1024], P(('dp', 'seq')), may hold values from -6 to 6
- segments: int32 [8, 512], P('dp'), may hold values from 0 to 2, never falling along the last dimension, each value on 1 to 256 neighbouring positions
- shared_params: float32 [9216], P(('dp', 'seq')), as said below
- split_params: float32 [4, 3146752], P('seq', 'dp'), as said below
- shared_m1: float32 [9216], P(('dp', 'seq')), may hold values from -56 to 56
- split_m1: float32 [4, 3146752], P('seq', 'dp'), may hold values from -56 to 56
- shared_m2: float32 [9216], P(('dp', 'seq')), may hold values from 204.8 to 819.2
- split_m2: float32 [4, 3146752], P('seq', 'dp'), may hold values from 204.8 to 819.2
Outputs:
- output: bfloat16 [4096, 1024], P(('dp', 'seq'))
- input_grad: float32 [4096, 1024], P(('dp', 'seq'))
- shared_grads: float32 [9216], P(('dp', 'seq'))
- split_grads: float32 [4, 3146752], P('seq', 'dp')
- shared_new: float32 [9216], P(('dp', 'seq'))
- split_new: float32 [4, 3146752], P('seq', 'dp')
- shared_m1_new: float32 [9216], P(('dp', 'seq'))
- split_m1_new: float32 [4, 3146752], P('seq', 'dp')
- shared_m2_new: float32 [9216], P(('dp', 'seq'))
- split_m2_new: float32 [4, 3146752], P('seq', 'dp')
Inputs may be any that keep to these rules, and one draw needn't show every extreme that they name: `shared_params`: the 9216 entries are the shared parameters packed as the first step reads them. `split_params`: row s holds the share s of the qkv, dense, fc and proj parameters as the second step reads them.
All inputs are finite; a program needn't handle non-finite values.
Results may differ from a plain program's by a relative error of at most 0.007.
The roundings to bfloat16 on the way count: a program that leaves them out, or rounds other values in their place, can miss the bound.
Values may be sent and summed in bfloat16 or wider, within the bound.
A program may use at most 192 MiB of HBM per device.

v0:
```python
import math

import jax
import jax.numpy as jnp
from jax import lax
from jax.sharding import PartitionSpec as P

MODEL_WIDTH = 1024
HEADS = 16
HEAD_DIM = 64
FF = 4096
ROT = 16
STEP = 3


norm_eps = 1e-05
beta_first = 0.9
beta_second = 0.95
adam_eps = 1e-08
learn_rate = 0.1
weight_decay = 0.01
rotary_base = 10000.0
masked_score = -1e30


def unpack_shared(flat_vec):
    extents = [
        (3 * MODEL_WIDTH,),
        (MODEL_WIDTH,),
        (MODEL_WIDTH,),
        (MODEL_WIDTH,),
        (MODEL_WIDTH,),
        (MODEL_WIDTH,),
        (MODEL_WIDTH,),
    ]
    pieces = []
    offset = 0
    for extent in extents:
        number = math.prod(extent)
        pieces.append(flat_vec[offset : offset + number])
        offset = offset + number
    return pieces


def unpack_split(matrix, seq_count):
    rows = matrix.shape[0]
    qkv_part = 3 * MODEL_WIDTH // seq_count
    dense_output_slice = MODEL_WIDTH // seq_count
    hidden_units_slice = FF // seq_count
    zero_end = MODEL_WIDTH * qkv_part
    first_end = zero_end + dense_output_slice * MODEL_WIDTH
    second_end = first_end + MODEL_WIDTH * hidden_units_slice
    third_end = second_end + hidden_units_slice
    w_qkv = (
        matrix[:, :zero_end]
        .reshape(rows, MODEL_WIDTH, qkv_part)
        .transpose(1, 0, 2)
        .reshape(MODEL_WIDTH, rows * qkv_part)
    )
    dense_weight = matrix[:, zero_end:first_end].reshape(rows * dense_output_slice, MODEL_WIDTH)
    expand_weight = (
        matrix[:, first_end:second_end]
        .reshape(rows, MODEL_WIDTH, hidden_units_slice)
        .transpose(1, 0, 2)
        .reshape(MODEL_WIDTH, rows * hidden_units_slice)
    )
    b_fc = matrix[:, second_end:third_end].reshape(rows * hidden_units_slice)
    contract_weight = matrix[:, third_end:].reshape(rows * hidden_units_slice, MODEL_WIDTH)
    return (w_qkv, dense_weight, expand_weight, b_fc, contract_weight)


def pack_split(w_qkv, dense_weight, expand_weight, b_fc, contract_weight, seq_count):
    qkv_part = 3 * MODEL_WIDTH // seq_count
    dense_output_slice = MODEL_WIDTH // seq_count
    hidden_units_slice = FF // seq_count
    rows = dense_weight.shape[0] // dense_output_slice
    return jnp.concatenate(
        [
            w_qkv.reshape(MODEL_WIDTH, rows, qkv_part)
            .transpose(1, 0, 2)
            .reshape(rows, MODEL_WIDTH * qkv_part),
            dense_weight.reshape(rows, dense_output_slice * MODEL_WIDTH),
            expand_weight.reshape(MODEL_WIDTH, rows, hidden_units_slice)
            .transpose(1, 0, 2)
            .reshape(rows, MODEL_WIDTH * hidden_units_slice),
            b_fc.reshape(rows, hidden_units_slice),
            contract_weight.reshape(rows, hidden_units_slice * MODEL_WIDTH),
        ],
        1,
    )


def adamw(param_vals, first_m, second_m, grad_vals):
    first_new = beta_first * first_m + (1.0 - beta_first) * grad_vals
    second_new = beta_second * second_m + (1.0 - beta_second) * grad_vals * grad_vals
    first_hat = first_new / (1.0 - beta_first**STEP)
    second_hat = second_new / (1.0 - beta_second**STEP)
    param_new = param_vals - learn_rate * (
        first_hat / (jnp.sqrt(second_hat) + adam_eps) + weight_decay * param_vals
    )
    return (param_new, first_new, second_new)


def layer_norm(resid, gain_vec, shift_vec):
    average = jnp.mean(resid, -1, keepdims=True)
    centered = resid - average
    variance = jnp.mean(centered * centered, -1, keepdims=True)
    recip_root = lax.rsqrt(variance + norm_eps)
    normed = centered * recip_root
    return (normed * gain_vec + shift_vec, normed, recip_root)


def norm_back(grad_norm, gain_vec, normed, recip_root):
    scaled = grad_norm * gain_vec
    return recip_root * (
        scaled
        - jnp.mean(scaled, -1, keepdims=True)
        - normed * jnp.mean(scaled * normed, -1, keepdims=True)
    )


def gelu_slope(inputs):
    normal_cdf = 0.5 * (1.0 + jax.scipy.special.erf(inputs * 0.7071067811865476))
    return normal_cdf + inputs * jnp.exp(-0.5 * inputs * inputs) * 0.3989422804014327


def rotary_tables(segment_row):
    indices = jnp.arange(segment_row.shape[0], dtype=jnp.int32)
    change = jnp.concatenate([jnp.ones((1,), dtype=jnp.bool_), segment_row[1:] != segment_row[:-1]])
    starts = lax.cummax(jnp.where(change, indices, jnp.zeros_like(indices)), axis=0)
    positions = (indices - starts).astype(jnp.float32)
    frequency = rotary_base ** (-jnp.arange(0, ROT, 2, dtype=jnp.float32) / ROT)
    angles = positions[:, None] * frequency[None, :]
    return (jnp.cos(angles)[:, None, :], jnp.sin(angles)[:, None, :])


def rotate(field, cosines, sines, direction):
    half_rot = ROT // 2
    first_half = field[..., :half_rot]
    second = field[..., half_rot:ROT]
    return jnp.concatenate(
        [
            first_half * cosines - direction * second * sines,
            second * cosines + direction * first_half * sines,
            field[..., ROT:],
        ],
        -1,
    )


def score_block(query_block, keys_rot, seg_block, row_ids, segment_row, col_ids):
    scale = HEAD_DIM ** (-0.5)
    scores = (
        jnp.einsum("ihd,jhd->hij", query_block, keys_rot, preferred_element_type=jnp.float32)
        * scale
    )
    allowed = (seg_block[:, None] == segment_row[None, :]) & (row_ids[:, None] >= col_ids[None, :])
    return jnp.where(allowed[None], scores, masked_score)


def attention_forward(queries, keys_rot, values, segment_row):
    segment_length, heads_here, head_size = queries.shape
    block_rows = min(512, segment_length)
    block_count = segment_length // block_rows
    col_ids = jnp.arange(segment_length, dtype=jnp.int32)

    def one_block(packed):
        query_block, seg_block, row_ids = packed
        scores = score_block(query_block, keys_rot, seg_block, row_ids, segment_row, col_ids)
        row_max = jnp.max(scores, -1, keepdims=True)
        log_total = row_max[..., 0] + jnp.log(jnp.sum(jnp.exp(scores - row_max), -1))
        probability = jnp.exp(scores - log_total[..., None]).astype(jnp.bfloat16)
        attended = jnp.einsum(
            "hij,jhd->ihd", probability, values, preferred_element_type=jnp.float32
        ).astype(jnp.bfloat16)
        return (attended, log_total)

    attended, log_totals = lax.map(
        one_block,
        (
            queries.reshape(block_count, block_rows, heads_here, head_size),
            segment_row.reshape(block_count, block_rows),
            col_ids.reshape(block_count, block_rows),
        ),
    )
    return (attended.reshape(segment_length, heads_here, head_size), log_totals)


def attention_backward(queries, keys_rot, values, attended, log_totals, grad_att, segment_row):
    segment_length, heads_here, head_size = queries.shape
    block_rows = min(512, segment_length)
    block_count = segment_length // block_rows
    col_ids = jnp.arange(segment_length, dtype=jnp.int32)
    scale = HEAD_DIM ** (-0.5)

    def one_block(running, packed):
        grad_keys, grad_values = running
        query_block, out_block, grad_block, log_total, seg_block, row_ids = packed
        scores = score_block(query_block, keys_rot, seg_block, row_ids, segment_row, col_ids)
        probability = jnp.exp(scores - log_total[..., None])
        prob_low = probability.astype(jnp.bfloat16)
        delta = jnp.sum(grad_block.astype(jnp.float32) * out_block.astype(jnp.float32), -1).T
        grad_values = grad_values + jnp.einsum(
            "hij,ihd->jhd", prob_low, grad_block, preferred_element_type=jnp.float32
        )
        grad_prob = jnp.einsum(
            "ihd,jhd->hij", grad_block, values, preferred_element_type=jnp.float32
        )
        grad_scores = (probability * (grad_prob - delta[..., None]) * scale).astype(jnp.bfloat16)
        grad_query = jnp.einsum(
            "hij,jhd->ihd", grad_scores, keys_rot, preferred_element_type=jnp.float32
        )
        grad_keys = grad_keys + jnp.einsum(
            "hij,ihd->jhd", grad_scores, query_block, preferred_element_type=jnp.float32
        )
        return ((grad_keys, grad_values), grad_query)

    zero_field = jnp.zeros((segment_length, heads_here, head_size), jnp.float32)
    shaped = (
        queries.reshape(block_count, block_rows, heads_here, head_size),
        attended.reshape(block_count, block_rows, heads_here, head_size),
        grad_att.reshape(block_count, block_rows, heads_here, head_size),
        log_totals,
        segment_row.reshape(block_count, block_rows),
        col_ids.reshape(block_count, block_rows),
    )
    (grad_keys, grad_values), grad_query = lax.scan(one_block, (zero_field, zero_field), shaped)
    return (grad_query.reshape(segment_length, heads_here, head_size), grad_keys, grad_values)


def local(
    hidden_in,
    cotangent,
    segments,
    shared_params,
    split_params,
    shared_m1,
    split_m1,
    shared_m2,
    split_m2,
):
    tokens_here = hidden_in.shape[0]
    seq_count = lax.axis_size("seq")
    heads_here = HEADS // seq_count
    qkv_cols = 3 * MODEL_WIDTH // seq_count
    shared_full = lax.all_gather(shared_params, ("dp", "seq"), axis=0, tiled=True)
    b_qkv, b_dense, b_proj, gain_one, shift_one, gain_two, shift_two = unpack_shared(shared_full)
    split_mine = lax.all_gather(split_params.astype(jnp.bfloat16), "dp", axis=1, tiled=True)
    w_qkv_share, dense_weight, expand_weight, b_fc, contract_weight = unpack_split(
        split_mine, seq_count
    )
    b_fc = b_fc.astype(jnp.float32)
    column_rows = lax.all_gather(split_mine[:, : MODEL_WIDTH * qkv_cols], "seq", axis=0, tiled=True)
    w_qkv = (
        column_rows.reshape(seq_count, MODEL_WIDTH, qkv_cols)
        .transpose(1, 0, 2)
        .reshape(MODEL_WIDTH, 3 * MODEL_WIDTH)
    )
    resid = hidden_in.astype(jnp.float32)
    first_norm, normed_one, root_one = layer_norm(resid, gain_one, shift_one)
    second_norm, normed_two, root_two = layer_norm(resid, gain_two, shift_two)
    first_low = first_norm.astype(jnp.bfloat16)
    second_low = second_norm.astype(jnp.bfloat16)
    group_first, group_norm, group_cot = (
        lax.all_gather(first_low, "seq", axis=0, tiled=True),
        lax.all_gather(second_low, "seq", axis=0, tiled=True),
        lax.all_gather(cotangent, "seq", axis=0, tiled=True),
    )
    group_length = group_first.shape[0]
    qkv = (
        (jnp.dot(first_low, w_qkv, preferred_element_type=jnp.float32) + b_qkv)
        .astype(jnp.bfloat16)
        .reshape(tokens_here, HEADS, 3 * HEAD_DIM)
    )
    grouped = lax.all_to_all(qkv, "seq", split_axis=1, concat_axis=0, tiled=True)
    segment_row = segments[0]
    cosines, sines = rotary_tables(segment_row)
    queries = rotate(grouped[..., :HEAD_DIM].astype(jnp.float32), cosines, sines, 1.0).astype(
        jnp.bfloat16
    )
    keys_rot = rotate(
        grouped[..., HEAD_DIM : 2 * HEAD_DIM].astype(jnp.float32), cosines, sines, 1.0
    ).astype(jnp.bfloat16)
    values = grouped[..., 2 * HEAD_DIM :]
    attended, log_totals = attention_forward(queries, keys_rot, values, segment_row)
    grad_outf = cotangent.astype(jnp.float32)
    grad_b_proj = jnp.sum(grad_outf, 0)
    grad_b_dense = jnp.sum(grad_outf, 0)
    att_flat = attended.reshape(group_length, heads_here * HEAD_DIM)
    hidden_pre = jnp.dot(group_norm, expand_weight, preferred_element_type=jnp.float32) + b_fc
    hidden_activations = jax.nn.gelu(hidden_pre, approximate=False).astype(jnp.bfloat16)
    branch = jnp.dot(att_flat, dense_weight, preferred_element_type=jnp.float32) + jnp.dot(
        hidden_activations, contract_weight, preferred_element_type=jnp.float32
    )
    total = (
        resid + lax.psum_scatter(branch, "seq", scatter_dimension=0, tiled=True) + b_dense + b_proj
    )
    output = total.astype(jnp.bfloat16)
    grad_w_proj = jnp.dot(hidden_activations.T, group_cot, preferred_element_type=jnp.float32)
    grad_hidden = jnp.dot(
        group_cot, contract_weight.T, preferred_element_type=jnp.float32
    ) * gelu_slope(hidden_pre)
    grad_b_fc = jnp.sum(grad_hidden, 0)
    hidden_reduced_precision = grad_hidden.astype(jnp.bfloat16)
    grad_w_fc = jnp.dot(group_norm.T, hidden_reduced_precision, preferred_element_type=jnp.float32)
    grad_second = lax.psum_scatter(
        jnp.dot(hidden_reduced_precision, expand_weight.T, preferred_element_type=jnp.float32),
        "seq",
        scatter_dimension=0,
        tiled=True,
    )
    grad_w_dense = jnp.dot(att_flat.T, group_cot, preferred_element_type=jnp.float32)
    grad_att_heads = (
        jnp.dot(group_cot, dense_weight.T, preferred_element_type=jnp.float32)
        .astype(jnp.bfloat16)
        .reshape(group_length, heads_here, HEAD_DIM)
    )
    grad_query, grad_keys, grad_values = attention_backward(
        queries, keys_rot, values, attended, log_totals, grad_att_heads, segment_row
    )
    grad_query = rotate(grad_query, cosines, sines, -1.0)
    grad_keys = rotate(grad_keys, cosines, sines, -1.0)
    grad_grouped = jnp.concatenate([grad_query, grad_keys, grad_values], -1).astype(jnp.bfloat16)
    grad_w_qkv_share = jnp.dot(
        group_first.T,
        grad_grouped.reshape(group_length, qkv_cols),
        preferred_element_type=jnp.float32,
    )
    grad_qkv = lax.all_to_all(grad_grouped, "seq", split_axis=0, concat_axis=1, tiled=True).reshape(
        tokens_here, 3 * MODEL_WIDTH
    )
    grad_b_qkv = jnp.sum(grad_qkv.astype(jnp.float32), 0)
    grad_first = jnp.dot(grad_qkv, w_qkv.T, preferred_element_type=jnp.float32)
    grad_gain_one = jnp.sum(grad_first * normed_one, 0)
    grad_shift_one = jnp.sum(grad_first, 0)
    grad_gain_two = jnp.sum(grad_second * normed_two, 0)
    grad_shift_two = jnp.sum(grad_second, 0)
    input_grad = (
        grad_outf
        + norm_back(grad_first, gain_one, normed_one, root_one)
        + norm_back(grad_second, gain_two, normed_two, root_two)
    )
    shared_flat = jnp.concatenate(
        [
            grad_b_qkv,
            grad_b_dense,
            grad_b_proj,
            grad_gain_one,
            grad_shift_one,
            grad_gain_two,
            grad_shift_two,
        ]
    )
    shared_grads = lax.psum_scatter(shared_flat, ("dp", "seq"), scatter_dimension=0, tiled=True)
    split_local = pack_split(
        grad_w_qkv_share, grad_w_dense, grad_w_fc, grad_b_fc, grad_w_proj, seq_count
    )
    split_grads = lax.psum_scatter(split_local, "dp", scatter_dimension=1, tiled=True)
    shared_new, shared_m1_new, shared_m2_new = adamw(
        shared_params, shared_m1, shared_m2, shared_grads
    )
    split_new, split_m1_new, split_m2_new = adamw(split_params, split_m1, split_m2, split_grads)
    return (
        output,
        input_grad,
        shared_grads,
        split_grads,
        shared_new,
        split_new,
        shared_m1_new,
        split_m1_new,
        shared_m2_new,
        split_m2_new,
    )


def solution(mesh):
    in_specs = (
        P(("dp", "seq"), None),
        P(("dp", "seq"), None),
        P("dp", None),
        P(("dp", "seq")),
        P("seq", "dp"),
        P(("dp", "seq")),
        P("seq", "dp"),
        P(("dp", "seq")),
        P("seq", "dp"),
    )
    out_specs = (
        P(("dp", "seq"), None),
        P(("dp", "seq"), None),
        P(("dp", "seq")),
        P("seq", "dp"),
        P(("dp", "seq")),
        P("seq", "dp"),
        P(("dp", "seq")),
        P("seq", "dp"),
        P(("dp", "seq")),
        P("seq", "dp"),
    )
    return jax.shard_map(local, mesh=mesh, in_specs=in_specs, out_specs=out_specs, check_vma=False)
```

profile of v0, /device:TPU:0, one launch (start us, length us, event | category | flops | bytes accessed | tf_op | source)
XLA Modules:
  0.0 872.5 jit_solution(2449875439309951270)
XLA Ops:
  7.2 4.1 convert_element_type.85
  11.7 45.1 %all-reduce = f32[9216]{0:T(1024)S(1)} all-reduce(f32[9216]{0:T(1024)S(1)} %dynamic-update-slice), channel_id=1, replica_groups=mesh['dp'=8,'seq'=4] {'dp','seq'}, use_global_device_ids=true, to_apply=%add | all-reduce | flops 9216 | bytes 73728
  57.3 1.1 fusion.32
  58.4 0.7 all-gather.11.cloned.1.call-update
  59.1 132.5 %all-gather.7.cloned.1.call-done = bf16[1,3146752]{1,0:T(2,128)(2,1)} async-done(((bf16[1,393344]{1,0:T(2,128)(2,1)}), bf16[1,3146752]{1,0:T(2,128)(2,1)}) %all-gather.7.cloned.1.call-update) | async-done | bytes 6293520 | tf_op jit(solution)/shard_map/all_gather | solution.py:248
  191.6 6.7 slice_bitcast_fusion
  198.4 0.5 all-gather.13.cloned.1.call-update
  199.4 0.3 reduce-window.9
  200.0 0.9 fusion.20
  201.0 47.0 %slice_reduce_fusion = (bf16[1048576]{0:T(1024)(128)(2,1)S(1)}, bf16[1048576]{0:T(1024)(128)(2,1)}) fusion(bf16[1,3146752]{1,0:T(2,128)(2,1)} %all-gather.7.cloned.1.call-done), kind=kLoop, calls=%fused_computation.1 | loop fusion | bytes 8388608 | tf_op jit(solution)/shard_map/slice | solution.py:68
  248.0 4.2 reshape_transpose_reshape.9
  252.2 0.7 slice_convert_fusion.2
  252.9 8.3 fusion.5
  261.2 10.2 %slice_reduce_fusion.2 = bf16[262144]{0:T(1024)(128)(2,1)S(1)} fusion(bf16[1,3146752]{1,0:T(2,128)(2,1)} %all-gather.7.cloned.1.call-done), kind=kLoop, calls=%fused_computation.53 | loop fusion | bytes 1048576 | tf_op jit(solution)/shard_map/slice | solution.py:60
  271.6 2.3 reshape.247
  273.9 4.5 fusion.65
  278.5 1.0 copy-done.20
  279.4 1.3 convolution_bitcast_fusion.1
  280.8 6.4 copy.90
  287.1 2.5 convolution_bitcast_fusion
  289.6 6.5 copy.91
  296.1 4.6 fusion.49
  300.7 9.9 %all-gather.15.cloned.1.call-done = bf16[4,1,786432]{2,1,0:T(2,128)(2,1)} async-done(((bf16[1,1,786432]{2,1,0:T(2,128)(2,1)}), bf16[4,1,786432]{2,1,0:T(2,128)(2,1)}) %all-gather.15.cloned.1.call-update) | async-done | bytes 6291472 | tf_op jit(solution)/shard_map/all_gather | solution.py:253
  310.6 41.8 %reduce.1 = bf16[4,786432]{1,0:T(4,128)(2,1)} reduce(bf16[4,1,786432]{2,1,0:T(2,128)(2,1)} %all-gather.15.cloned.1.call-done, bf16[]{:T(256)} %constant.183), dimensions={1}, to_apply=%all-gather.reduce_sub_computation | reduce | bytes 12582914 | tf_op jit(solution)/shard_map/all_gather | solution.py:253
  352.4 6.2 copy.94
  358.6 8.7 copy.65
  367.3 5.0 fusion.1
  372.3 1.2 copy.66
  373.5 3.5 all-to-all-start
  377.2 1.2 convolution_convert_fusion
  378.4 4.5 fusion.66
  382.9 5.7 all-to-all-done
  389.0 0.6 copy-done.7
  389.6 0.9 fusion.2
  390.5 0.9 exponential_reduce_fusion
  391.4 1.3 multiply_reduce_fusion
  392.8 1.6 multiply_convert_fusion
  394.4 0.7 convolution_bitcast_fusion.5
  395.1 0.5 convolution_bitcast_fusion.6
  395.8 1.3 fusion.19
  397.1 2.5 convolution_bitcast_fusion.2
  399.6 3.5 copy.88
  403.1 2.8 constant_dynamic-update-slice_fusion.5
  405.9 0.4 convolution_bitcast_fusion.3
  406.4 1.1 copy.89
  407.5 1.8 convolution_add_fusion.1
  409.4 1.0 constant_dynamic-update-slice_fusion.4
  410.4 7.3 constant_dynamic-update-slice_fusion.3
  417.7 0.6 constant_dynamic-update-slice_fusion.2
  418.3 3.6 constant_dynamic-update-slice_fusion.1
  421.9 1.1 copy-done.11
  423.0 1.4 copy.73
  424.4 3.5 all-to-all-start.1
  428.0 0.6 dynamic-slice.4
  429.2 21.8 %all-to-all-done.1 = bf16[512,4,192]{2,1,0:T(4,128)(2,1)S(1)} async-done(((bf16[512,4,192]{2,1,0:T(4,128)(2,1)}), bf16[512,4,192]{2,1,0:T(4,128)(2,1)S(1)}, u32[]{:S(2)}, u32[]{:S(2)}) %all-to-all-start.1) | async-done | bytes 786464 | tf_op jit(solution)/shard_map/all_to_all | solution.py:329
  451.0 1.4 copy.82
  452.4 0.9 convert_reduce_fusion
  453.6 0.7 copy.75
  454.4 4.2 fusion.42
  458.7 2.7 convert_reduce_fusion.2
  461.5 43.6 %all-reduce.1 = f32[9216]{0:T(1024)S(1)} all-reduce(f32[9216]{0:T(1024)S(1)} %constant_dynamic-update-slice_fusion.6), channel_id=4, replica_groups=mesh['dp'=8,'seq'=4] {'dp','seq'}, use_global_device_ids=true, to_apply=%region_19.20.clone | all-reduce | flops 9216 | bytes 73728
  505.1 0.7 multiply_subtract_fusion.1
  505.8 346.8 %all-reduce.5.cloned.1.call-done = f32[1,3146752]{1,0:T(1,128)} async-done(((f32[1,3146752]{1,0:T(1,128)}), f32[1,3146752]{1,0:T(1,128)}) %all-reduce.5.cloned.1.call-update) | async-done | bytes 12587024
  852.5 12.8 %multiply_subtract_fusion = (f32[1,393344]{1,0:T(1,128)}, f32[1,393344]{1,0:T(1,128)}, f32[1,393344]{1,0:T(1,128)}, f32[1,393344]{1,0:T(1,128)}) fusion(f32[1,393344]{1,0:T(1,128)S(1)} %copy-done.2, f32[1,393344]{1,0:T(1,128)} %param.15, f32[1,393344]{1,0:T(1,128)} %param.17, f32[1,3146752]{1,0:T(1,128)} %all-reduce.5.cloned.1.call-done, u32[]{:T(128)S(6)} %multiply.59), kind=kLoop, calls=%fused_computation.43 | loop fusion | flops 5900160 | bytes 12587012 | tf_op jit(solution)/shard_map/sub | solution.py:98
  (98 shorter events, 3.3 us)
Async XLA Ops:
  7.2 4.3 copy-start.14
  7.2 49.7 %copy-start.1 = (bf16[128,1024]{1,0:T(8,128)(2,1)S(1)}, bf16[128,1024]{1,0:T(8,128)(2,1)}, u32[]{:S(2)}) copy-start(bf16[128,1024]{1,0:T(8,128)(2,1)} %param.9) | copy-start | bytes 786436
  7.2 184.4 %all-gather.7.cloned.1.call-start = ((), (), s32[]{:S(2)}) async-start(), calls=%async_computation.4 | async-start | bytes 14160384 | tf_op jit(solution)/shard_map/all_gather | solution.py:248
  11.4 241.5 %all-gather.9.cloned.1.call-start = ((), (), s32[]{:S(2)}) async-start(), calls=%async_computation.5 | async-start | bytes 1310720 | tf_op jit(solution)/shard_map/all_gather | solution.py:266
  56.9 142.3 %copy-start.12 = (f32[9216]{0:T(1024)}, f32[9216]{0:T(1024)S(1)}, u32[]{:S(2)}) copy-start(f32[9216]{0:T(1024)S(1)} %all-reduce) | copy-start | bytes 110596
  58.3 215.6 %all-gather.11.cloned.1.call-start = ((), (), s32[]{:S(2)}) async-start(), calls=%async_computation.7 | async-start | bytes 1310720 | tf_op jit(solution)/shard_map/all_gather | solution.py:267
  59.1 251.5 %all-gather.15.cloned.1.call-start = ((), (), s32[]{:S(2)}) async-start(), calls=%async_computation.10 | async-start | bytes 15728640 | tf_op jit(solution)/shard_map/all_gather | solution.py:253
  198.3 0.9 copy-start.13
  198.3 198.7 %all-gather.13.cloned.1.call-start = ((), (), s32[]{:S(2)}) async-start(), calls=%async_computation.9 | async-start | bytes 1310720 | tf_op jit(solution)/shard_map/all_gather | solution.py:265
  198.9 255.4 %reduce-scatter.6.cloned.1.call-start = ((), (), s32[]{:S(2)}) async-start(), calls=%async_computation.8 | async-start | bytes 2621440 | tf_op jit(solution)/shard_map/reduce_scatter | solution.py:306
  273.9 5.5 copy-start.17
  278.5 1.0 copy-start.20
  280.8 6.4 copy-start.8
  358.6 8.7 copy-start.3
  358.6 8.7 slice-start
  373.5 15.1 %all-to-all-start = ((bf16[128,16,192]{0,2,1:T(8,128)(2,1)}), bf16[128,16,192]{0,2,1:T(8,128)(2,1)S(1)}, u32[]{:S(2)}, u32[]{:S(2)}) async-start(bf16[128,16,192]{0,2,1:T(8,128)(2,1)} %bitcast.3), calls=%async_computation | async-start | bytes 1572864 | tf_op jit(solution)/shard_map/all_to_all | solution.py:275
  377.0 81.7 %reduce-scatter.4.cloned.1.call-start = ((), (), s32[]{:S(2)}) async-start(), calls=%async_computation.6 | async-start | bytes 2621440 | tf_op jit(solution)/shard_map/reduce_scatter | solution.py:296
  388.6 1.0 copy-start.7
  390.5 1.0 copy-start.18
  397.0 2.6 copy-start.10
  403.1 2.8 copy-start.9
  405.9 1.6 copy-start.4
  409.3 443.2 %all-reduce.5.cloned.1.call-start = ((), (), s32[]{:S(2)}) async-start(), calls=%async_computation.11 | async-start | bytes 25174016
  410.4 7.9 copy-start
  421.9 1.1 copy-start.11
  423.0 5.0 copy-start.19
  424.4 26.6 %all-to-all-start.1 = ((bf16[512,4,192]{2,1,0:T(4,128)(2,1)}), bf16[512,4,192]{2,1,0:T(4,128)(2,1)S(1)}, u32[]{:S(2)}, u32[]{:S(2)}) async-start(bf16[512,4,192]{2,1,0:T(4,128)(2,1)} %copy.73), calls=%async_computation.2 | async-start | bytes 2097152 | tf_op jit(solution)/shard_map/all_to_all | solution.py:329
  454.3 4.3 copy-start.5
  454.4 4.3 copy-start.6
  458.6 46.5 %copy-start.15 = (f32[288]{0:T(512)S(1)}, f32[288]{0:T(512)}, u32[]{:S(2)}) copy-start(f32[288]{0:T(512)} %param.14) | copy-start | bytes 3460
  458.6 46.5 %copy-start.16 = (f32[288]{0:T(512)S(1)}, f32[288]{0:T(512)}, u32[]{:S(2)}) copy-start(f32[288]{0:T(512)} %param.16) | copy-start | bytes 3460
  458.6 393.9 %copy-start.2 = (f32[1,393344]{1,0:T(1,128)S(1)}, f32[1,393344]{1,0:T(1,128)}, u32[]{:S(2)}) copy-start(f32[1,393344]{1,0:T(1,128)} %param.13) | copy-start | bytes 4720132
Sparse Core Ops, SparseCore 0:
  11.5 180.1 all-gather.6
  193.8 14.8 all-gather.8
  210.3 16.7 all-gather.10
  228.5 82.0 all-gather.14
  312.6 16.7 all-gather.12
  331.7 31.4 reduce-scatter.5
  409.4 40.0 reduce-scatter.3
  453.6 398.8 all-reduce.4
where the time goes:
time: 876 us; the launch traced here: 872 us
  waiting for transfers between devices  518 us (59%)
  local copies, waits for them, and re-layouts  127 us (14%)
  blocking collectives  88.7 us (10%)
  other arithmetic  67.9 us (8%)
  matrix products  47.2 us (5%)
  between operations  15.6 us (2%)
    unnamed x9, waiting for transfers between devices  348 us
    all_gather x1, waiting for transfers between devices, local(): lax.all_gather(split_params.astype(jnp.bfloat16), 'dp', axis=1, tiled=True)  133 us
    unnamed x2, blocking collectives  88.7 us
    slice x1, local copies, waits for them, and re-layouts, unpack_split(): matrix[:, third_end:].reshape(rows * hidden_units_slice, MODEL_WIDTH)  47 us
    unnamed x63, local copies, waits for them, and re-layouts  45.8 us
    all_gather x1, other arithmetic, local(): lax.all_gather(split_mine[:, :MODEL_WIDTH * qkv_cols], 'seq', axis=0, til...  41.8 us
    all_to_all x1, waiting for transfers between devices, local(): lax.all_to_all(grad_grouped, 'seq', split_axis=0, concat_axis=1, tiled=True)  21.8 us
  transfers between devices with their start and end apart: 10, of which 5 were waited for; matrix products, arithmetic and copies ran while one was open for 26% of the time, Pallas kernels for 0%

commit v1 on v0

--- a/solution.py
+++ b/solution.py
@@ -228,7 +228,7 @@
     return (grad_query.reshape(segment_length, heads_here, head_size), grad_keys, grad_values)
 
 
-def local(
+def local_general(
     hidden_in,
     cotangent,
     segments,
@@ -374,6 +374,204 @@
     )
 
 
+LANES = 128
+
+
+def share_layout(seq_count):
+    ql = 3 * MODEL_WIDTH // seq_count
+    dl = MODEL_WIDTH // seq_count
+    fl = FF // seq_count
+    return [
+        MODEL_WIDTH * ql // LANES,
+        dl * MODEL_WIDTH // LANES,
+        MODEL_WIDTH * fl // LANES,
+        fl // LANES,
+        fl * MODEL_WIDTH // LANES,
+    ]
+
+
+def gather_parts(split_params, shared_params, dp_count, seq_count):
+    rows = split_params.shape[1] // LANES
+    mine = split_params.reshape(rows, LANES).astype(jnp.bfloat16)
+    mine = jnp.pad(mine, ((0, -rows % 16), (0, 0)))
+    blocks = lax.all_gather(mine, "dp", axis=0, tiled=False)
+    full = blocks[:, :rows].reshape(dp_count * rows, LANES)
+    shared_full = lax.all_gather(shared_params, ("dp", "seq"), axis=0, tiled=True)
+    return full, shared_full
+
+
+def reduce_parts(flat, shared_flat, dp_count, seq_count):
+    rows = flat.shape[0] // dp_count
+    blocks = flat.reshape(dp_count, rows, LANES)
+    got = lax.all_to_all(blocks, "dp", split_axis=0, concat_axis=0, tiled=True)
+    grads = jnp.sum(got.astype(jnp.float32), 0).reshape(1, rows * LANES)
+    shared = lax.psum_scatter(shared_flat, ("dp", "seq"), scatter_dimension=0, tiled=True)
+    return grads, shared
+
+
+def attend(queries, keys_rot, values, segment_row):
+    length = queries.shape[1]
+    ids = jnp.arange(length, dtype=jnp.int32)
+    allowed = (segment_row[:, None] == segment_row[None, :]) & (ids[:, None] >= ids[None, :])
+    scores = jnp.einsum("hid,hjd->hij", queries, keys_rot, preferred_element_type=jnp.float32)
+    scores = jnp.where(allowed[None], scores * HEAD_DIM ** (-0.5), masked_score)
+    row_max = jnp.max(scores, -1, keepdims=True)
+    log_total = row_max + jnp.log(jnp.sum(jnp.exp(scores - row_max), -1, keepdims=True))
+    prob = jnp.exp(scores - log_total)
+    prob_low = prob.astype(jnp.bfloat16)
+    attended = jnp.einsum("hij,hjd->hid", prob_low, values, preferred_element_type=jnp.float32)
+    return attended.astype(jnp.bfloat16), prob, prob_low
+
+
+def attend_back(queries, keys_rot, values, attended, prob, prob_low, grad_att):
+    delta = jnp.sum(grad_att.astype(jnp.float32) * attended.astype(jnp.float32), -1, keepdims=True)
+    grad_values = jnp.einsum("hij,hid->hjd", prob_low, grad_att, preferred_element_type=jnp.float32)
+    grad_prob = jnp.einsum("hid,hjd->hij", grad_att, values, preferred_element_type=jnp.float32)
+    grad_scores = (prob * (grad_prob - delta) * HEAD_DIM ** (-0.5)).astype(jnp.bfloat16)
+    grad_query = jnp.einsum(
+        "hij,hjd->hid", grad_scores, keys_rot, preferred_element_type=jnp.float32
+    )
+    grad_keys = jnp.einsum("hij,hid->hjd", grad_scores, queries, preferred_element_type=jnp.float32)
+    return grad_query, grad_keys, grad_values
+
+
+def local_grouped(
+    hidden_in,
+    cotangent,
+    segments,
+    shared_params,
+    split_params,
+    shared_m1,
+    split_m1,
+    shared_m2,
+    split_m2,
+):
+    dp_count = lax.axis_size("dp")
+    seq_count = lax.axis_size("seq")
+    share = lax.axis_index("seq")
+    heads_here = HEADS // seq_count
+    ql = 3 * MODEL_WIDTH // seq_count
+    dl = MODEL_WIDTH // seq_count
+    fl = FF // seq_count
+    f32, bf16 = jnp.float32, jnp.bfloat16
+    tokens_here = hidden_in.shape[0]
+    both = lax.all_gather(
+        jnp.concatenate([hidden_in, cotangent], 1), "seq", axis=0, tiled=True
+    )
+    group_hidden, group_cot = both[:, :MODEL_WIDTH], both[:, MODEL_WIDTH:]
+    full, shared_full = gather_parts(split_params, shared_params, dp_count, seq_count)
+    b_qkv, b_dense, b_proj, gain_one, shift_one, gain_two, shift_two = unpack_shared(shared_full)
+    extents = share_layout(seq_count)
+    offsets = [sum(extents[:k]) for k in range(6)]
+    w_qkv, w_dense, w_fc, b_fc, w_proj = [
+        full[offsets[k] : offsets[k + 1]].reshape(shape)
+        for k, shape in enumerate(
+            [(MODEL_WIDTH, ql), (dl, MODEL_WIDTH), (MODEL_WIDTH, fl), (fl,), (fl, MODEL_WIDTH)]
+        )
+    ]
+    b_fc = b_fc.astype(f32)
+    b_qkv_mine = lax.dynamic_slice(b_qkv, (share * ql,), (ql,))
+
+    resid = group_hidden.astype(f32)
+    first_norm, normed, root = layer_norm(resid, gain_one, shift_one)
+    first_low = first_norm.astype(bf16)
+    second_low = (normed * gain_two + shift_two).astype(bf16)
+    length = resid.shape[0]
+
+    qkv = (jnp.dot(first_low, w_qkv, preferred_element_type=f32) + b_qkv_mine).astype(bf16)
+    qkv = qkv.reshape(length, heads_here, 3, HEAD_DIM).transpose(2, 1, 0, 3)
+    segment_row = segments[0]
+    cosines, sines = rotary_tables(segment_row)
+    cosines, sines = cosines[:, 0], sines[:, 0]
+    queries = rotate(qkv[0].astype(f32), cosines, sines, 1.0).astype(bf16)
+    keys_rot = rotate(qkv[1].astype(f32), cosines, sines, 1.0).astype(bf16)
+    values = qkv[2]
+    attended, prob, prob_low = attend(queries, keys_rot, values, segment_row)
+    att_flat = attended.transpose(1, 0, 2).reshape(length, dl)
+
+    hidden_pre = jnp.dot(second_low, w_fc, preferred_element_type=f32) + b_fc
+    activated = jax.nn.gelu(hidden_pre, approximate=False).astype(bf16)
+    branch = jnp.dot(att_flat, w_dense, preferred_element_type=f32) + jnp.dot(
+        activated, w_proj, preferred_element_type=f32
+    )
+    total = lax.psum_scatter(branch, "seq", scatter_dimension=0, tiled=True)
+    output = (hidden_in.astype(f32) + total + b_dense + b_proj).astype(bf16)
+
+    grad_outf = cotangent.astype(f32)
+    grad_b_out = jnp.sum(grad_outf, 0)
+    grad_w_proj = jnp.dot(activated.T, group_cot, preferred_element_type=f32)
+    grad_hidden = jnp.dot(group_cot, w_proj.T, preferred_element_type=f32) * gelu_slope(hidden_pre)
+    grad_b_fc = jnp.sum(grad_hidden, 0)
+    grad_hidden_low = grad_hidden.astype(bf16)
+    grad_w_fc = jnp.dot(second_low.T, grad_hidden_low, preferred_element_type=f32)
+    grad_second = jnp.dot(grad_hidden_low, w_fc.T, preferred_element_type=f32)
+    grad_w_dense = jnp.dot(att_flat.T, group_cot, preferred_element_type=f32)
+    grad_att = (
+        jnp.dot(group_cot, w_dense.T, preferred_element_type=f32)
+        .astype(bf16)
+        .reshape(length, heads_here, HEAD_DIM)
+        .transpose(1, 0, 2)
+    )
+    grad_query, grad_keys, grad_values = attend_back(
+        queries, keys_rot, values, attended, prob, prob_low, grad_att
+    )
+    grad_query = rotate(grad_query, cosines, sines, -1.0)
+    grad_keys = rotate(grad_keys, cosines, sines, -1.0)
+    grad_qkv = (
+        jnp.stack([grad_query, grad_keys, grad_values])
+        .astype(bf16)
+        .transpose(2, 1, 0, 3)
+        .reshape(length, ql)
+    )
+    grad_b_qkv = jnp.sum(grad_qkv.astype(f32), 0)
+    grad_w_qkv = jnp.dot(first_low.T, grad_qkv, preferred_element_type=f32)
+    grad_first = jnp.dot(grad_qkv, w_qkv.T, preferred_element_type=f32)
+
+    scaled = lax.psum_scatter(
+        gain_one * grad_first + gain_two * grad_second, "seq", scatter_dimension=0, tiled=True
+    )
+    normed_mine = lax.dynamic_slice(normed, (share * tokens_here, 0), (tokens_here, MODEL_WIDTH))
+    root_mine = lax.dynamic_slice(root, (share * tokens_here, 0), (tokens_here, 1))
+    input_grad = grad_outf + norm_back(scaled, 1.0, normed_mine, root_mine)
+
+    shared_flat = jnp.concatenate(
+        [
+            lax.dynamic_update_slice(
+                jnp.zeros((3 * MODEL_WIDTH,), f32), grad_b_qkv, (share * ql,)
+            ),
+            grad_b_out,
+            grad_b_out,
+            jnp.sum(grad_first * normed, 0),
+            jnp.sum(grad_first, 0),
+            jnp.sum(grad_second * normed, 0),
+            jnp.sum(grad_second, 0),
+        ]
+    )
+    flat = jnp.concatenate(
+        [
+            part.astype(bf16).reshape(-1, LANES)
+            for part in (grad_w_qkv, grad_w_dense, grad_w_fc, grad_b_fc, grad_w_proj)
+        ]
+    )
+    split_grads, shared_grads = reduce_parts(flat, shared_flat, dp_count, seq_count)
+    shared_new, shared_m1_new, shared_m2_new = adamw(
+        shared_params, shared_m1, shared_m2, shared_grads
+    )
+    split_new, split_m1_new, split_m2_new = adamw(split_params, split_m1, split_m2, split_grads)
+    return (
+        output,
+        input_grad,
+        shared_grads,
+        split_grads,
+        shared_new,
+        split_new,
+        shared_m1_new,
+        split_m1_new,
+        shared_m2_new,
+        split_m2_new,
+    )
+
+
 def solution(mesh):
     in_specs = (
         P(("dp", "seq"), None),
@@ -398,4 +596,7 @@
         P(("dp", "seq")),
         P("seq", "dp"),
     )
+    dp_count, seq_count = mesh.shape["dp"], mesh.shape["seq"]
+    even = sum(share_layout(seq_count)) % dp_count == 0
+    local = local_grouped if even else local_general
     return jax.shard_map(local, mesh=mesh, in_specs=in_specs, out_specs=out_specs, check_vma=False)

time: 876 us -> 433 us (0.49)
  waiting for transfers between devices: 518 us -> 90.1 us
  blocking collectives: 88.7 us -> 159 us
  local copies, waits for them, and re-layouts: 127 us -> 63.9 us
  other arithmetic: 67.9 us -> 49 us
    unnamed x9 -> x4, waiting for transfers between devices: 348 us -> 0.07 us
    all_gather x5 -> x2, waiting for transfers between devices: 142 us -> 63.4 us  [the longest x1 63.4 us: gather_parts(): blocks = lax.all_gather(mine, 'dp', axis=0, tiled=False)]
    unnamed x2, blocking collectives: 88.7 us -> 159 us
    slice x3 -> x7, local copies, waits for them, and re-layouts: 57.2 us -> 11.7 us  [the longest x1 5.86 us: gather_parts(): full = blocks[:, :rows].reshape(dp_count * rows, LANES)]
    all_gather x1 -> x0, other arithmetic: 41.8 us -> none  [local(): lax.all_gather(split_mine[:, :MODEL_WIDTH * qkv_cols], 'seq', axis=0, til...]
    unnamed x63 -> x64, local copies, waits for them, and re-layouts: 45.8 us -> 12.1 us
    reshape x2 -> x11, local copies, waits for them, and re-layouts: 2.54 us -> 35.6 us  [the longest x4 11.7 us: local_grouped(): part.astype(bf16).reshape(-1, LANES)]
    all_to_all x2 -> x1, waiting for transfers between devices: 27.5 us -> 0.01 us  [reduce_parts(): got = lax.all_to_all(blocks, 'dp', split_axis=0, concat_axis=0, tiled=True)]
  transfers between devices with their start and end apart: 10 -> 5, of which waited for: 5 -> 2; matrix products, arithmetic and copies ran while one was open for 26% -> 9% of each run, Pallas kernels for 0% -> 0%
where the time goes in v1:
time: 433 us; the launch traced here: 424 us
  blocking collectives  159 us (37%)
  waiting for transfers between devices  90.1 us (21%)
  local copies, waits for them, and re-layouts  63.9 us (15%)
  other arithmetic  49 us (11%)
  matrix products  42.7 us (10%)
  between operations  14.8 us (3%)
  starting transfers between devices  5.04 us (1%)
    unnamed x2, blocking collectives  159 us
    all_gather x1, waiting for transfers between devices, gather_parts(): blocks = lax.all_gather(mine, 'dp', axis=0, tiled=False)  63.4 us
    reduce_scatter x1, waiting for transfers between devices, local_grouped(): lax.psum_scatter(gain_one * grad_first + gain_two * grad_second, 'seq', s...  26.6 us
    convert_element_type x1, other arithmetic, gather_parts(): mine = split_params.reshape(rows, LANES).astype(jnp.bfloat16)  16.3 us
    sub x2, other arithmetic, adamw(): param_vals - learn_rate * (first_hat / (jnp.sqrt(second_hat) + adam_eps)...  14.4 us
    unnamed x64, local copies, waits for them, and re-layouts  12.1 us
    reshape x4, local copies, waits for them, and re-layouts, local_grouped(): part.astype(bf16).reshape(-1, LANES)  11.7 us
    reshape x4, local copies, waits for them, and re-layouts, local_grouped(): full[offsets[k]:offsets[k + 1]].reshape(shape)  9.25 us
  transfers between devices with their start and end apart: 5, of which 2 were waited for; matrix products, arithmetic and copies ran while one was open for 9% of the time, Pallas kernels for 0%

profile of v1, /device:TPU:0, one launch (start us, length us, event | category | flops | bytes accessed | tf_op | source)
XLA Modules:
  0.0 424.5 jit_solution(1324723384844046410)
XLA Ops:
  7.2 2.0 pad_maximum_fusion
  9.3 16.3 %convert_reduce_fusion.2 = bf16[393344]{0:T(1024)(128)(2,1)S(1)} fusion(f32[1,393344]{1,0:T(1,128)S(1)} %copy-done.1), kind=kLoop, calls=%fused_computation.51 | loop fusion | flops 393344 | bytes 2360064 | tf_op jit(solution)/shard_map/convert_element_type | solution.py:395
  25.7 0.9 pad.4
  26.7 0.3 dynamic-update-slice
  26.9 43.7 %all-reduce.1 = f32[9216]{0:T(1024)S(1)} all-reduce(f32[9216]{0:T(1024)S(1)} %dynamic-update-slice), channel_id=1, replica_groups=mesh['dp'=8,'seq'=4] {'dp','seq'}, use_global_device_ids=true, to_apply=%add.1 | all-reduce | flops 9216 | bytes 73728
  70.8 0.3 reduce-window.9
  71.9 1.4 convert_reduce_fusion.1
  73.4 1.6 fusion.4
  75.0 63.4 %all-gather.6.cloned.1.call-done = bf16[24704,128]{1,0:T(8,128)(2,1)} async-done(((bf16[3088,128]{1,0:T(8,128)(2,1)}), bf16[24704,128]{1,0:T(8,128)(2,1)}) %all-gather.6.cloned.1.call-update) | async-done | bytes 6324240 | tf_op jit(solution)/shard_map/all_gather | solution.py:397
  138.5 5.9 %slice.146 = bf16[8,3073,128]{2,1,0:T(8,128)(2,1)} slice(bf16[8,3088,128]{2,1,0:T(8,128)(2,1)} %bitcast.79), slice={[0:8], [0:3073], [0:128]} | slice | bytes 12587008 | tf_op jit(solution)/shard_map/slice | solution.py:398
  144.3 7.3 %reshape.308 = bf16[24584,128]{1,0:T(8,128)(2,1)} reshape(bf16[8,3073,128]{2,1,0:T(8,128)(2,1)} %slice.146) | data formatting | bytes 12587008 | tf_op jit(solution)/shard_map/reshape | solution.py:398
  151.6 0.7 fusion.34
  152.3 4.5 %fusion.47 = (bf16[8192,128]{1,0:T(8,128)(2,1)}, bf16[8192,128]{1,0:T(8,128)(2,1)}) fusion(bf16[24584,128]{1,0:T(8,128)(2,1)} %reshape.308), kind=kLoop, calls=%fused_computation.136 | loop fusion | bytes 8388608 | tf_op jit(solution)/shard_map/slice | solution.py:467
  156.7 1.0 slice-done
  158.0 0.3 slice-done.1
  158.3 2.4 reshape.309
  160.7 2.9 add_convert_fusion.2
  164.2 0.9 fusion.1
  165.1 0.9 exponential_reduce_fusion
  166.0 0.7 copy-done.3
  166.7 0.5 convolution_convert_fusion.6
  167.2 1.3 multiply_reduce_fusion.3
  168.5 2.0 fusion.21
  170.5 1.6 multiply_convert_fusion
  172.1 0.5 fusion.30
  172.6 1.5 fusion.32
  174.1 4.3 %reshape.314 = bf16[1024,1024]{1,0:T(8,128)(2,1)} reshape(bf16[8192,128]{1,0:T(8,128)(2,1)} %get-tuple-element.27) | data formatting | bytes 4194304 | tf_op jit(solution)/shard_map/reshape | solution.py:467
  178.4 2.3 reshape.315
  180.8 1.1 slice.225
  181.9 0.9 subtract_convert_fusion.1
  183.1 0.9 copy-done.15
  184.0 0.6 copy-done.4
  184.7 2.5 convolution_convert_fusion.2
  187.1 3.2 reshape.318
  190.4 1.2 constant_dynamic-update-slice_fusion.5
  191.6 0.9 copy-done.5
  192.5 1.3 convolution_convert_fusion.3
  193.8 1.3 reshape.319
  195.1 8.3 %fusion.7 = (bf16[512,1024]{1,0:T(8,128)(2,1)}, f32[512,1024]{1,0:T(8,128)S(1)}) fusion(f32[1024]{0:T(1024)S(1)} %fusion.34, bf16[1024,1024]{1,0:T(8,128)(2,1)} %reshape.314, f32[1024]{0:T(1024)S(1)} %get-tuple-element.45, f32[1024]{0:T(1024)S(1)} %get-tuple-element.46, f32[512]{0:T(512)S(1)} %add_rsqrt_fusion, f32[512]{0:T(512)S(1)} %broadcast_multiply_fusion.1, ...), kind=kOutput, calls=%fused_computation.17 | convolution fusion | flops 1111490560 | bytes 6307840 | tf_op jit(solution)/shard_map/dot_general | solution.py:492
  203.4 2.2 fusion.49
  205.6 1.0 copy-done.24
  206.6 2.8 convolution_convert_fusion.1
  209.3 4.2 reshape.320
  213.5 3.8 convolution_convert_fusion
  217.3 3.1 reshape.321
  220.4 0.9 constant_dynamic-update-slice_fusion.4
  221.2 3.1 constant_dynamic-update-slice_fusion.3
  224.4 0.5 constant_dynamic-update-slice_fusion.2
  224.9 1.4 constant_dynamic-update-slice_fusion.1
  226.3 7.3 %reshape.322 = bf16[8,3073,128]{2,1,0:T(8,128)(2,1)} reshape(bf16[24584,128]{1,0:T(8,128)(2,1)} %constant_dynamic-update-slice_fusion.1) | data formatting | bytes 12587008 | tf_op jit(solution)/shard_map/reshape | solution.py:405
  233.6 4.9 %all-to-all-start = ((bf16[8,3073,128]{2,1,0:T(8,128)(2,1)}), bf16[8,3073,128]{2,1,0:T(8,128)(2,1)}, u32[]{:S(2)}, u32[]{:S(2)}) async-start(bf16[8,3073,128]{2,1,0:T(8,128)(2,1)} %reshape.322), calls=%async_computation.2 | async-start | bytes 12615680 | tf_op jit(solution)/shard_map/all_to_all | solution.py:406
  238.6 2.6 fusion.51
  241.5 3.9 multiply_reduce_fusion
  245.4 1.5 copy-done.9
  246.9 2.5 fusion.50
  249.4 1.8 convolution_add_fusion
  251.7 26.6 %reduce-scatter.5.cloned.1.call-done = f32[128,1024]{1,0:T(8,128)} async-done(((f32[512,1024]{1,0:T(8,128)}), f32[128,1024]{1,0:T(8,128)}) %reduce-scatter.5.cloned.1.call-update) | async-done | bytes 524304 | tf_op jit(solution)/shard_map/reduce_scatter | solution.py:530
  278.3 1.3 fusion.44
  279.7 2.2 convert_reduce_fusion.4
  281.9 115.1 %all-reduce.2 = f32[9216]{0:T(1024)S(1)} all-reduce(f32[9216]{0:T(1024)S(1)} %constant_dynamic-update-slice_fusion.6), channel_id=5, replica_groups=mesh['dp'=8,'seq'=4] {'dp','seq'}, use_global_device_ids=true, to_apply=%region_17.18.clone | all-reduce | flops 9216 | bytes 73728
  397.0 0.7 multiply_subtract_fusion.1
  397.7 1.8 add_convert_fusion.3
  399.6 4.0 convert_reduce_fusion
  403.7 13.7 %multiply_subtract_fusion = (f32[1,393344]{1,0:T(1,128)}, f32[1,393344]{1,0:T(1,128)}, f32[1,393344]{1,0:T(1,128)}, f32[1,393344]{1,0:T(1,128)}) fusion(f32[1,393344]{1,0:T(1,128)S(1)} %copy-done.2, f32[1,393344]{1,0:T(1,128)S(1)} %copy-done.11, f32[1,393344]{1,0:T(1,128)S(1)} %copy-done.12, f32[1,1,3073,128]{3,2,1,0:T(8,128)S(1)} %bitcast.78), kind=kLoop, calls=%fused_computation.49 | loop fusion | flops 5900160 | bytes 12587008 | tf_op jit(solution)/shard_map/sub | solution.py:98
  (100 shorter events, 3.3 us)
Async XLA Ops:
  7.2 2.1 copy-start.1
  7.2 64.7 %all-gather.4.cloned.1.call-start = ((), (), s32[]{:S(2)}) async-start(), calls=%async_computation.3 | async-start | bytes 2621440 | tf_op jit(solution)/shard_map/all_gather | solution.py:458
  9.2 17.4 %copy-start.21 = (f32[288]{0:T(512)S(1)}, f32[288]{0:T(512)}, u32[]{:S(2)}) copy-start(f32[288]{0:T(512)} %param.12) | copy-start | bytes 3460
  9.2 61.4 %copy-start.20 = (s32[1,512]{1,0:T(1,128)S(1)}, s32[1,512]{1,0:T(1,128)}, u32[]{:S(2)}) copy-start(s32[1,512]{1,0:T(1,128)} %param.11) | copy-start | bytes 6148
  9.3 129.2 %all-gather.6.cloned.1.call-start = ((), (), s32[]{:S(2)}) async-start(), calls=%async_computation.6 | async-start | bytes 7114752 | tf_op jit(solution)/shard_map/all_gather | solution.py:397
  156.7 1.0 slice-start
  156.7 1.6 slice-start.1
  165.1 1.6 copy-start.3
  168.5 23.1 %copy-start.17 = (bf16[4,512,64]{1,2,0:T(8,128)(2,1)}, bf16[4,512,64]{1,2,0:T(8,128)(2,1)S(1)}, u32[]{:S(2)}) copy-start(bf16[4,512,64]{1,2,0:T(8,128)(2,1)S(1)} %get-tuple-element.62) | copy-start | bytes 786436
  174.1 4.3 %copy-start = (bf16[8192,128]{1,0:T(8,128)(2,1)S(1)}, bf16[8192,128]{1,0:T(8,128)(2,1)}, u32[]{:S(2)}) copy-start(bf16[8192,128]{1,0:T(8,128)(2,1)} %get-tuple-element.26) | copy-start | bytes 6291460
  180.8 2.1 copy-start.19
  182.8 1.9 copy-start.4
  183.1 0.9 copy-start.15
  190.4 2.2 copy-start.5
  191.6 3.4 copy-start.6
  195.1 8.3 %copy-start.8 = (bf16[1024,1024]{1,0:T(8,128)(2,1)S(1)}, bf16[1024,1024]{1,0:T(8,128)(2,1)}, u32[]{:S(2)}) copy-start(bf16[1024,1024]{1,0:T(8,128)(2,1)} %reshape.315) | copy-start | bytes 6291460
  205.6 1.0 copy-start.24
  233.6 5.0 %copy-start.16 = (bf16[512,4,3,64]{0,3,2,1:T(8,128)(2,1)S(1)}, bf16[512,4,3,64]{0,3,2,1:T(8,128)(2,1)}, u32[]{:S(2)}) copy-start(bf16[512,4,3,64]{0,3,2,1:T(8,128)(2,1)} %copy-done.15) | copy-start | bytes 2359300
  233.6 165.9 %all-to-all-start = ((bf16[8,3073,128]{2,1,0:T(8,128)(2,1)}), bf16[8,3073,128]{2,1,0:T(8,128)(2,1)}, u32[]{:S(2)}, u32[]{:S(2)}) async-start(bf16[8,3073,128]{2,1,0:T(8,128)(2,1)} %reshape.322), calls=%async_computation.2 | async-start | bytes 12615680 | tf_op jit(solution)/shard_map/all_to_all | solution.py:406
  238.5 2.7 copy-start.7
  238.5 39.8 %reduce-scatter.5.cloned.1.call-start = ((), (), s32[]{:S(2)}) async-start(), calls=%async_computation.5 | async-start | bytes 2621440 | tf_op jit(solution)/shard_map/reduce_scatter | solution.py:530
  238.6 2.6 copy-start.10
  238.6 2.9 copy-start.25
  245.4 1.6 copy-start.9
  245.4 4.0 copy-start.18
  245.4 152.3 %reduce-scatter.3.cloned.1.call-start = ((), (), s32[]{:S(2)}) async-start(), calls=%async_computation.4 | async-start | bytes 2621440 | tf_op jit(solution)/shard_map/reduce_scatter | solution.py:497
  251.2 28.4 %copy-start.13 = (bf16[128,1024]{1,0:T(8,128)(2,1)S(1)}, bf16[128,1024]{1,0:T(8,128)(2,1)}, u32[]{:S(2)}) copy-start(bf16[128,1024]{1,0:T(8,128)(2,1)} %param.10) | copy-start | bytes 786436
  251.2 145.8 %copy-start.22 = (f32[288]{0:T(512)S(1)}, f32[288]{0:T(512)}, u32[]{:S(2)}) copy-start(f32[288]{0:T(512)} %param.14) | copy-start | bytes 3460
  251.2 145.8 %copy-start.23 = (f32[288]{0:T(512)S(1)}, f32[288]{0:T(512)}, u32[]{:S(2)}) copy-start(f32[288]{0:T(512)} %param.16) | copy-start | bytes 3460
  251.2 146.5 %copy-start.14 = (bf16[128,1024]{1,0:T(8,128)(2,1)S(1)}, bf16[128,1024]{1,0:T(8,128)(2,1)}, u32[]{:S(2)}) copy-start(bf16[128,1024]{1,0:T(8,128)(2,1)} %param.9) | copy-start | bytes 786436
  399.5 4.0 copy-start.2
  399.5 4.0 copy-start.11
  399.6 4.2 copy-start.12
Sparse Core Ops, SparseCore 0:
  10.2 25.2 all-gather.3
  38.2 100.1 all-gather.5
  245.5 32.7 reduce-scatter.4
  280.8 31.3 reduce-scatter.2
